TPU v7x, 1024 devices: a whole 4x4x32 slice. The times are simulated.
1024 devices in a mesh: dp: 4 (over x), expert: 64 (over z, y_hi), pipe: 4 (over y_lo, core).
Axes of the slice: x: 4, y: 4 (y_hi: 2, y_lo: 2; y = y_hi * 2 + y_lo), z: 32, core: 2. Of those that a mesh axis runs over, the one named last changes fastest.
Arguments:
- dout: bfloat16 [8192, 4096], P('expert', ('dp', 'pipe')), may hold values from -6 to 6
- expert_ids: int32 [8192, 8], P('expert'), may hold values from 0 to 63, all different within a row; in each aligned block of 128 rows (0 to 127, 128 to 255, ...) at most 20 rows name the same one
- gates: bfloat16 [8192, 8], P('expert'), may hold values from 0.049804688 to 0.5
- down_weight: bfloat16 [64, 1536, 4096], P('expert', None, ('dp', 'pipe')), may hold values from -0.15625 to 0.15625
- hidden_stash: bfloat16 [64, 1280, 1536], P('expert'), may hold values from -0.29882812 to 0.29882812
Outputs:
- hidden_grad: bfloat16 [64, 1280, 1536], P('expert', ('dp', 'pipe'))
- down_grad: bfloat16 [64, 1536, 4096], P('expert', None, ('dp', 'pipe'))
- gate_grad: float32 [8192, 8], P('expert')
Inputs may be any that keep to these rules, and one draw needn't show every extreme that they name: `expert_ids`: among the pairs of the 128 tokens of one block no expert is named more than 20 times, and in every draw some expert is named exactly 20 times in some block; the 8 choices of a token differ.
All inputs are finite; a program needn't handle non-finite values.
Results may differ from a plain program's by a relative error of at most 0.022.
Values may be sent and summed in bfloat16 or wider, within the bound.
A program may use at most 32 MiB of HBM per device.

v0:
```python
import jax
import jax.numpy as jnp
from jax import lax
from jax.sharding import PartitionSpec as P


def local(dout, expert_ids, gates, down_weight, hidden_stash):
    tok_count, top_count = expert_ids.shape
    local_experts, slot_total, width_hidden = hidden_stash.shape
    senders = lax.axis_size("expert")
    capacity = slot_total // senders
    total_experts = local_experts * senders
    width_local = dout.shape[1]
    flat_ids = expert_ids.reshape(-1)
    onehot = (flat_ids[:, None] == jnp.arange(total_experts, dtype=jnp.int32)[None, :]).astype(
        jnp.int32
    )
    slot_index = jnp.sum(jnp.cumsum(onehot, axis=0) * onehot, axis=1) - 1
    target = flat_ids * capacity + slot_index
    scaled = (gates.astype(jnp.float32)[:, :, None] * dout.astype(jnp.float32)[:, None, :]).astype(
        jnp.bfloat16
    )
    values = scaled.reshape(-1, width_local)
    empty = jnp.zeros((total_experts * capacity, values.shape[1]), values.dtype)
    arrived = lax.all_to_all(
        empty.at[target].set(values).reshape(senders, local_experts * capacity, values.shape[1]),
        "expert",
        split_axis=0,
        concat_axis=0,
        tiled=True,
    )
    shaped = arrived.reshape(senders, local_experts, capacity, arrived.shape[-1])
    routed = shaped.transpose(1, 0, 2, 3).reshape(
        local_experts, senders * capacity, arrived.shape[-1]
    )
    summed = lax.psum_scatter(
        jnp.einsum("erd,efd->ref", routed, down_weight, preferred_element_type=jnp.float32).astype(
            jnp.bfloat16
        ),
        ("dp", "pipe"),
        scatter_dimension=0,
        tiled=True,
    )
    hidden_grad = summed.transpose(1, 0, 2)
    down_grad = jnp.einsum(
        "erf,erd->efd", hidden_stash, routed, preferred_element_type=jnp.float32
    ).astype(jnp.bfloat16)
    expert_out = jnp.einsum(
        "erf,efd->erd", hidden_stash, down_weight, preferred_element_type=jnp.float32
    ).astype(jnp.bfloat16)
    shaped = expert_out.reshape(local_experts, senders, capacity, expert_out.shape[-1])
    returned = lax.all_to_all(
        shaped.transpose(1, 0, 2, 3).reshape(
            senders, local_experts * capacity, expert_out.shape[-1]
        ),
        "expert",
        split_axis=0,
        concat_axis=0,
        tiled=True,
    )
    returned = returned.reshape(total_experts * capacity, width_local)
    picked = returned[target].reshape(tok_count, top_count, width_local)
    partial_value = jnp.einsum("tkd,td->tk", picked, dout, preferred_element_type=jnp.float32)
    gate_grad = lax.psum(partial_value, ("dp", "pipe"))
    return (hidden_grad, down_grad, gate_grad)


def solution(mesh):
    in_specs = (
        P("expert", ("dp", "pipe")),
        P("expert", None),
        P("expert", None),
        P("expert", None, ("dp", "pipe")),
        P("expert", None, None),
    )
    out_specs = (
        P("expert", ("dp", "pipe"), None),
        P("expert", None, ("dp", "pipe")),
        P("expert", None),
    )
    return jax.shard_map(local, mesh=mesh, in_specs=in_specs, out_specs=out_specs, check_vma=False)
```

profile of v0, /device:TPU:1, one launch (start us, length us, event | category | flops | bytes accessed | tf_op | source)
XLA Modules:
  0.0 294.5 jit_solution(11043671194367847829)
XLA Ops:
  7.2 0.0 copy-start
  7.2 0.0 reduce-scatter.2.cloned.1.call-start
  7.2 0.9 copy.10
  8.1 0.1 eq.29
  8.2 0.1 eq.25
  8.3 0.7 broadcast_multiply_fusion
  9.0 18.0 %reduce-window.6 = s32[64,8,128]{2,1,0:T(8,128)S(1)} reduce-window(s32[64,8,128]{2,1,0:T(8,128)S(1)} %fusion.26, s32[]{:T(128)} %constant.4.clone.1), window={size=1x1x128 pad=0_0x0_0x127_0}, to_apply=%region_0.0 | reduce-window | flops 8323072 | bytes 524292 | tf_op jit(solution)/shard_map/reduce-window
  27.0 0.1 slice.10
  27.1 0.1 copy.12
  27.3 0.1 copy.13
  27.4 0.1 broadcast_add_fusion
  27.5 0.1 fusion.25
  27.6 0.1 copy.9
  27.7 0.1 mul.41
  27.8 0.8 convert_element_type.39
  28.7 0.8 copy.14
  29.5 0.1 reshape.101
  29.6 5.6 %scatter_custom_fusion = bf16[1280,256]{1,0:T(8,128)(2,1)S(1)} fusion(s32[1024]{0:T(1024)S(1)} %bitcast.58, f32[128,256]{1,0:T(8,128)S(1)} %convert_element_type.39, f32[1024]{0:T(1024)S(1)} %reshape.101, bf16[]{:T(256)} %constant.5.clone.1), kind=kCustom, calls=%fused_computation.15 | custom fusion | flops 524288 | bytes 790530 | tf_op jit(solution)/shard_map/scatter | solution.py:26
  35.2 0.1 reshape.95
  35.3 117.5 %all_to_all.10 = bf16[64,20,256]{2,1,0:T(8,128)(2,1)S(1)} all-to-all(bf16[64,20,256]{2,1,0:T(8,128)(2,1)S(1)} %reshape.95), channel_id=1, replica_groups=mesh['dp'=4,'expert'=64,'pipe'=4] {'expert'}, dimensions={0} | all-to-all | bytes 1310720 | tf_op jit(solution)/shard_map/all_to_all | solution.py:25
  152.8 0.1 reshape.96
  153.0 0.0 copy-done
  153.0 3.1 %fusion = bf16[1280,1,1536]{2,0,1:T(8,128)(2,1)} fusion(bf16[1280,256]{1,0:T(8,128)(2,1)S(1)} %reshape.96, bf16[1,1536,256]{2,1,0:T(8,128)(2,1)S(1)} %copy-done), kind=kOutput, calls=%fused_computation.3 | convolution fusion | flops 1008599040 | bytes 5373952 | tf_op jit(solution)/shard_map/erd,efd->ref/dot_general | solution.py:37
  156.1 0.0 reduce-scatter.2.cloned.1.call-update
  156.1 3.3 %fusion.8 = bf16[1280,256]{1,0:T(8,128)(2,1)S(1)} fusion(bf16[1,1280,1536]{2,1,0:T(8,128)(2,1)} %param.9, bf16[1,1536,256]{2,1,0:T(8,128)(2,1)S(1)} %copy-done), kind=kOutput, calls=%fused_computation.9 | convolution fusion | flops 1006960640 | bytes 5373952 | tf_op jit(solution)/shard_map/erf,efd->erd/dot_general | solution.py:48
  159.4 1.0 reshape_transpose_reshape.4
  160.4 7.4 %all-to-all-start.1 = ((bf16[64,20,256]{2,1,0:T(8,128)(2,1)}), bf16[64,20,256]{2,1,0:T(8,128)(2,1)S(1)}, u32[]{:S(2)}, u32[]{:S(2)}) async-start(bf16[64,20,256]{2,1,0:T(8,128)(2,1)} %reshape_transpose_reshape.4), calls=%async_computation.2 | async-start | bytes 1572864 | tf_op jit(solution)/shard_map/all_to_all | solution.py:52
  167.8 3.3 %fusion.11 = bf16[1,1536,256]{1,2,0:T(8,128)(2,1)S(1)} fusion(bf16[1280,256]{1,0:T(8,128)(2,1)S(1)} %reshape.96, bf16[1,1280,1536]{2,1,0:T(8,128)(2,1)} %param.9), kind=kOutput, calls=%fused_computation.10 | convolution fusion | flops 1007026176 | bytes 5373952 | tf_op jit(solution)/shard_map/erf,erd->efd/dot_general | solution.py:45
  171.1 0.0 copy-start.1
  171.1 1.2 copy.15
  172.3 80.6 %all-to-all-done.1 = bf16[64,20,256]{2,1,0:T(8,128)(2,1)S(1)} async-done(((bf16[64,20,256]{2,1,0:T(8,128)(2,1)}), bf16[64,20,256]{2,1,0:T(8,128)(2,1)S(1)}, u32[]{:S(2)}, u32[]{:S(2)}) %all-to-all-start.1) | async-done | bytes 655392 | tf_op jit(solution)/shard_map/all_to_all | solution.py:52
  252.9 0.1 reshape.99
  253.1 3.9 %gather_fusion = bf16[1024,256]{1,0:T(8,128)(2,1)S(1)} fusion(bf16[1280,256]{1,0:T(8,128)(2,1)S(1)} %reshape.99, s32[1024]{0:T(1024)S(1)} %broadcast_clamp_fusion), kind=kCustom, calls=%fused_computation | custom fusion | bytes 1052672 | tf_op jit(solution)/shard_map/gather | solution.py:62
  257.0 0.0 copy-done.1
  257.0 0.3 fusion.19
  257.4 30.3 %psum.7 = f32[128,8]{0,1:T(8,128)} all-reduce(f32[128,8]{0,1:T(8,128)S(1)} %bitcast.61), channel_id=1, replica_groups=mesh['dp'=4,'expert'=64,'pipe'=4] {'dp','pipe'}, use_global_device_ids=true, to_apply=%region_5.6 | all-reduce | flops 1024 | bytes 8192 | tf_op jit(solution)/shard_map/psum | solution.py:64
  287.6 0.0 reduce-scatter.2.cloned.1.call-done
  (7 shorter events, 0.1 us)
Async XLA Ops:
  7.2 145.8 %copy-start = (bf16[1,1536,256]{2,1,0:T(8,128)(2,1)S(1)}, bf16[1,1536,256]{2,1,0:T(8,128)(2,1)}, u32[]{:S(2)}) copy-start(bf16[1,1536,256]{2,1,0:T(8,128)(2,1)} %param.8) | copy-start | bytes 2359300
  7.2 280.5 %reduce-scatter.2.cloned.1.call-start = ((), (), s32[]{:S(2)}) async-start(), calls=%async_computation.3 | async-start | bytes 4177920 | tf_op jit(solution)/shard_map/reduce_scatter | solution.py:36
  160.4 92.5 %all-to-all-start.1 = ((bf16[64,20,256]{2,1,0:T(8,128)(2,1)}), bf16[64,20,256]{2,1,0:T(8,128)(2,1)S(1)}, u32[]{:S(2)}, u32[]{:S(2)}) async-start(bf16[64,20,256]{2,1,0:T(8,128)(2,1)} %reshape_transpose_reshape.4), calls=%async_computation.2 | async-start | bytes 1572864 | tf_op jit(solution)/shard_map/all_to_all | solution.py:52
  171.1 85.9 %copy-start.1 = (bf16[128,256]{1,0:T(8,128)(2,1)S(1)}, bf16[128,256]{1,0:T(8,128)(2,1)}, u32[]{:S(2)}) copy-start(bf16[128,256]{1,0:T(8,128)(2,1)} %param.5) | copy-start | bytes 196612
Sparse Core Ops, SparseCore 0:
  156.2 68.1 reduce-scatter.1
where the time goes:
time: 295 us; the launch traced here: 294 us
  blocking collectives  148 us (50%)
  waiting for transfers between devices  80.7 us (27%)
  other arithmetic  25.4 us (9%)
  between operations  14.2 us (5%)
  matrix products  9.98 us (3%)
  local copies, waits for them, and re-layouts  9.03 us (3%)
  starting transfers between devices  7.42 us (3%)
    all_to_all x1, blocking collectives, local(): lax.all_to_all(empty.at[target].set(values).reshape(senders, local_expert...  118 us
    all_to_all x1, waiting for transfers between devices, local(): lax.all_to_all(shaped.transpose(1, 0, 2, 3).reshape(senders, local_expert...  80.6 us
    psum x1, blocking collectives, local(): gate_grad = lax.psum(partial_value, ('dp', 'pipe'))  30.3 us
    another operation x3, other arithmetic  18.2 us
    all_to_all x1, starting transfers between devices, local(): lax.all_to_all(shaped.transpose(1, 0, 2, 3).reshape(senders, local_expert...  7.38 us
  transfers between devices with their start and end apart: 2, of which 1 were waited for; matrix products, arithmetic and copies ran while one was open for 4% of the time, Pallas kernels for 0%

commit v1 on v0

v1 whole, which is shorter than its diff:
```python
import functools

import jax
import jax.numpy as jnp
from jax import lax
from jax.experimental import pallas as pl
from jax.experimental.pallas import tpu as pltpu
from jax.sharding import PartitionSpec as P

MESH = pl.DeviceIdType.MESH
F32 = jnp.float32
BF16 = jnp.bfloat16
NZ = 32
HALF = NZ // 2
TOK = 128
CAP = 20
ROWS = 4 * CAP
PACK = 48
META = 16
CHUNKS = ((0, 64), (64, 64 + META))


def iota(shape, dim):
    return lax.broadcasted_iota(jnp.int32, shape, dim)


def kernel(
    dout_ref, ids_ref, gates_ref, w_hbm, st_hbm, hg_ref, dg_ref, gg_ref,
    blk, w_v, st_v, rt, ys, yr, eo, pb, cr, xs, xr, yb, srow, rtab, ar,
    load_sem, ring_s, ring_r, y_s, y_r, c_s, c_r, x_s, x_r, b_s, b_r, sc_s, sc_r, ar_s, ar_r,
):
    dp, e, p = lax.axis_index("dp"), lax.axis_index("expert"), lax.axis_index("pipe")
    z, yh = lax.div(e, 2), lax.rem(e, 2)
    yl, core = lax.div(p, 2), lax.rem(p, 2)
    me = dp * 4 + p
    partner = z * 2 + (1 - yh)
    width = w_v.shape[0]
    cols = dout_ref.shape[1]
    halfw = width // 2

    load_w = pltpu.make_async_copy(w_hbm, w_v, load_sem.at[0])
    load_s = pltpu.make_async_copy(st_hbm, st_v, load_sem.at[1])
    load_w.start()
    load_s.start()

    barrier = pltpu.get_barrier_semaphore()

    def greet_expert(b, carry):
        @pl.when(b != e)
        def _():
            pl.semaphore_signal(barrier, inc=1, device_id=(dp, b, p), device_id_type=MESH)
        return carry

    def greet_group(i, carry):
        @pl.when(i != me)
        def _():
            pl.semaphore_signal(
                barrier, inc=1, device_id=(lax.div(i, 4), e, lax.rem(i, 4)), device_id_type=MESH
            )
        return carry

    lax.fori_loop(0, 2 * NZ, greet_expert, 0)
    lax.fori_loop(0, 16, greet_group, 0)

    ids_f = ids_ref[...].astype(F32)
    gates_f = gates_ref[...].astype(F32)
    meta = jnp.concatenate([ids_f, gates_f], axis=0).astype(BF16)
    blk[z, 0:TOK, :] = dout_ref[...]
    blk[z, TOK:TOK + META, 0:128] = meta
    blk[z, TOK:TOK + META, 128:cols] = jnp.zeros((META, cols - 128), BF16)

    pl.semaphore_wait(barrier, 2 * NZ - 1 + 15)

    def ring_copy(d, s, q):
        zz = lax.rem(z - (s - 1) + NZ, NZ) if d == 0 else lax.rem(z + (s - 1), NZ)
        to = lax.rem(z + 1, NZ) if d == 0 else lax.rem(z + NZ - 1, NZ)
        ref = blk.at[zz, pl.ds(*CHUNKS[q])]
        return pltpu.make_async_remote_copy(
            src_ref=ref, dst_ref=ref, send_sem=ring_s.at[d, s - 1, q], recv_sem=ring_r.at[d, s - 1, q],
            device_id=(dp, to * 2 + yh, p), device_id_type=MESH,
        )

    def ring_arrival(d, s, q):
        zz = lax.rem(z - s + NZ, NZ) if d == 0 else lax.rem(z + s, NZ)
        ref = blk.at[zz, pl.ds(*CHUNKS[q])]
        return pltpu.make_async_remote_copy(
            src_ref=ref, dst_ref=ref, send_sem=ring_s.at[d, s - 1, q], recv_sem=ring_r.at[d, s - 1, q],
            device_id=(dp, e, p), device_id_type=MESH,
        )

    for q in range(2):
        for d in range(2):
            ring_copy(d, 1, q).start()

    load_w.wait()
    load_s.wait()

    def out_rows(i, carry):
        r = pl.multiple_of(i * 320, 320)
        prod = jnp.dot(st_v[pl.ds(r, 320), :], w_v[...], preferred_element_type=F32)
        eo[pl.ds(i * 4, 4)] = prod.reshape(4, ROWS, cols)
        return carry

    lax.fori_loop(0, 4, out_rows, 0)

    lower_tri = (iota((TOK, TOK), 0) < iota((TOK, TOK), 1)).astype(F32).astype(BF16)
    rows80 = iota((ROWS, TOK), 0).astype(F32)
    rows48 = iota((PACK, TOK), 0).astype(F32)
    c_id, r_id = iota((ROWS, PACK), 1), iota((ROWS, PACK), 0)
    spot = jnp.where(c_id < CAP, c_id, c_id + CAP) + (1 - yh) * CAP
    place = jnp.where((c_id < 2 * CAP) & (spot == r_id), 1.0, 0.0).astype(BF16)
    yh_f = (yh * CAP).astype(F32)

    def group_of(s):
        up = lax.rem(z + s, 2) == 1
        low = jnp.where(up, lax.rem(z + s - 1, NZ), lax.rem(z - s + NZ, NZ))
        return lax.div(low, 2)

    def receive(s):
        for q in range(2):
            for d in range(2):
                def take():
                    ring_arrival(d, s, q).wait_recv()

                    @pl.when(s < (HALF if q == d else HALF - 1))
                    def _():
                        ring_copy(d, s + 1, q).start()

                if q == d:
                    take()
                else:
                    pl.when(s < HALF)(take)

    def y_copy(g):
        return pltpu.make_async_remote_copy(
            src_ref=ys.at[g], dst_ref=yr.at[g], send_sem=y_s.at[g], recv_sem=y_r.at[g],
            device_id=(dp, partner, p), device_id_type=MESH,
        )

    def select(s):
        g = group_of(s)
        x = blk[pl.ds(2 * g, 2), 0:TOK, :].reshape(2 * TOK, cols)
        match, gate = [], []
        for name in (e, partner):
            for j in range(2):
                m16 = blk[2 * g + j, TOK:TOK + META, 0:128].astype(F32)
                hit = m16[0:8] == name.astype(F32)
                match.append(jnp.sum(jnp.where(hit, 1.0, 0.0), axis=0, keepdims=True))
                gate.append(jnp.sum(jnp.where(hit, m16[8:16], 0.0), axis=0, keepdims=True))
        counts = jnp.dot(
            jnp.concatenate(match + [jnp.zeros((12, TOK), F32)], axis=0).astype(BF16),
            lower_tri, preferred_element_type=F32,
        )
        own, theirs = [], []
        for j in range(2):
            key = jnp.where(match[j] > 0.5, counts[j:j + 1] + (2.0 * j * CAP + yh_f), -1.0)
            own.append(jnp.where(rows80 == key, gate[j], 0.0))
            key = jnp.where(match[2 + j] > 0.5, counts[2 + j:3 + j] + 1.0 * j * CAP, -1.0)
            theirs.append(jnp.where(rows48 == key, gate[2 + j], 0.0))
        both = jnp.concatenate(
            [jnp.concatenate(own, axis=1), jnp.concatenate(theirs, axis=1)], axis=0
        ).astype(BF16)
        picked = jnp.dot(both, x, preferred_element_type=F32).astype(BF16)
        ys[g] = picked[ROWS:]
        y_copy(g).start()
        rt[g] = picked[:ROWS]

    def core_copy(g):
        h = lax.div(g, 2)
        return pltpu.make_async_remote_copy(
            src_ref=pb.at[g], dst_ref=cr.at[h], send_sem=c_s.at[h], recv_sem=c_r.at[h],
            device_id=(dp, e, yl * 2 + (1 - core)), device_id_type=MESH,
        )

    def score_copy(g, b):
        return pltpu.make_async_remote_copy(
            src_ref=srow.at[g], dst_ref=rtab.at[e], send_sem=sc_s, recv_sem=sc_r,
            device_id=(dp, b, p), device_id_type=MESH,
        )

    diagonal = iota((ROWS, 128), 0) == iota((ROWS, 128), 1)

    def multiply(s):
        g = group_of(s)
        y_copy(g).wait_recv()
        rr = (
            rt[g].astype(F32) + jnp.dot(place, yr[g], preferred_element_type=F32)
        ).astype(BF16)
        rt[g] = rr
        for n in range(width // 256):
            part = lax.dot_general(
                rr, w_v[n * 256:(n + 1) * 256, :], (((1,), (1,)), ((), ())),
                preferred_element_type=F32,
            )
            pb[g, :, n * 256:(n + 1) * 256] = part.astype(BF16)

        @pl.when(lax.rem(g, 2) != core)
        def _():
            core_copy(g).start()

        total = jnp.sum(rr.astype(F32) * eo[g], axis=1, keepdims=True)
        srow[g] = jnp.sum(jnp.where(diagonal, total, 0.0), axis=0, keepdims=True)
        for j in range(4):
            b = 4 * g + j

            @pl.when(b != e)
            def _():
                score_copy(g, b).start()

            @pl.when(b == e)
            def _():
                rtab[e] = srow[g]

    def x_copy(h, side, lo, size):
        to = lax.rem(dp + 1, 4) if side == 0 else lax.rem(dp + 3, 4)
        part = pl.ds(lo, size)
        return pltpu.make_async_remote_copy(
            src_ref=xs.at[h, :, part], dst_ref=xr.at[side, h, :, part],
            send_sem=x_s.at[side, h], recv_sem=x_r.at[side, h],
            device_id=(to, e, p), device_id_type=MESH,
        )

    b_copy = pltpu.make_async_remote_copy(
        src_ref=xs.at[lax.div(dp * 4 + 2 * (1 - yl) + core, 2)], dst_ref=yb, send_sem=b_s, recv_sem=b_r,
        device_id=(dp, e, 2 * (1 - yl) + core), device_id_type=MESH,
    )

    def add_up(dst, g, extra):
        h = lax.div(g, 2)
        for n in range(4):
            c = slice(n * (width // 4), (n + 1) * (width // 4))
            t = pb[g, :, c].astype(F32) + cr[h, :, c].astype(F32)
            for side, lo, hi in extra:
                if lo <= n * (width // 4) < hi:
                    t = t + xr[side, h, :, c].astype(F32)
            dst(c, t)

    def send_dst(h):
        def put(c, t):
            xs[h, :, c] = t.astype(BF16)
        return put

    def far(s):
        g = group_of(s)
        h = lax.div(g, 2)
        mine = lax.rem(g, 2) == core
        away = lax.rem(dp - lax.div(g, 4) + 4, 4)

        @pl.when(mine)
        def _():
            core_copy(g).wait_recv()

        @pl.when(mine & (away == 2))
        def _():
            add_up(send_dst(h), g, ())
            x_copy(h, 0, 0, halfw).start()
            x_copy(h, 1, halfw, halfw).start()

    def near(s):
        g = group_of(s)
        h = lax.div(g, 2)
        mine = lax.rem(g, 2) == core
        away = lax.rem(dp - lax.div(g, 4) + 4, 4)

        @pl.when(mine & (away == 1))
        def _():
            x_copy(h, 1, halfw, halfw).wait_recv()
            add_up(send_dst(h), g, ((1, halfw, width),))
            x_copy(h, 1, 0, width).start()

        @pl.when(mine & (away == 3))
        def _():
            x_copy(h, 0, 0, halfw).wait_recv()
            add_up(send_dst(h), g, ((0, 0, halfw),))
            x_copy(h, 0, 0, width).start()

    def column(s):
        g = group_of(s)
        h = lax.div(g, 2)
        mine = lax.rem(g, 2) == core
        away = lax.rem(dp - lax.div(g, 4) + 4, 4)

        @pl.when(mine & (away == 0))
        def _():
            x_copy(h, 0, 0, width).wait_recv()
            x_copy(h, 1, 0, width).wait_recv()

            @pl.when(lax.div(lax.rem(g, 4), 2) != yl)
            def _():
                add_up(send_dst(h), g, ((0, 0, width), (1, 0, width)))
                b_copy.start()

    last = HALF + 1

    def body(s, carry):
        @pl.when(s <= HALF)
        def _():
            receive(s)
            select(s)

        @pl.when(s >= 2)
        def _():
            multiply(s - 1)

        @pl.when(s >= 3)
        def _():
            far(s - 2)

        @pl.when(s >= 4)
        def _():
            near(s - 3)

        @pl.when(s >= 5)
        def _():
            column(s - 4)

        return carry

    lax.fori_loop(1, last + 1, body, 0)

    def down(lo, hi):
        for n in range(lo, hi):
            part = lax.dot_general(
                st_v[:, n * 256:(n + 1) * 256], rt[...].reshape(16 * ROWS, cols),
                (((0,), (0,)), ((), ())), preferred_element_type=F32,
            )
            dg_ref[0, n * 256:(n + 1) * 256, :] = part.astype(BF16)

    far(HALF)
    near(HALF - 1)
    column(HALF - 2)
    down(0, 3)
    near(HALF)
    column(HALF - 1)
    down(3, 6)
    column(HALF)

    pltpu.make_async_copy(
        rtab.at[pl.ds(0, 2 * NZ - 1)], rtab.at[pl.ds(0, 2 * NZ - 1)], sc_r
    ).wait()
    table = rtab[...].reshape(2 * NZ, 128)
    high = table.astype(BF16)
    low = (table - high.astype(F32)).astype(BF16)
    names = iota((2 * NZ, TOK), 0)
    hits = [jnp.where(names == ids_ref[k:k + 1, :], 1.0, 0.0) for k in range(8)]
    named = functools.reduce(lambda a, b: a + b, hits)
    counts = jnp.dot(named.astype(BF16), lower_tri, preferred_element_type=F32)
    lanes = iota((128, TOK), 0).astype(F32)
    first = (lax.rem(e, 4) * CAP).astype(F32)
    out = []
    for k in range(8):
        slot = jnp.sum(hits[k] * counts, axis=0, keepdims=True) + first
        one = hits[k].astype(BF16)
        values = lax.dot_general(
            high, one, (((0,), (0,)), ((), ())), preferred_element_type=F32
        ) + lax.dot_general(low, one, (((0,), (0,)), ((), ())), preferred_element_type=F32)
        out.append(jnp.sum(jnp.where(lanes == slot, values, 0.0), axis=0, keepdims=True))
    ar[me] = jnp.concatenate(out, axis=0)

    def spread(i):
        return pltpu.make_async_remote_copy(
            src_ref=ar.at[me], dst_ref=ar.at[me], send_sem=ar_s, recv_sem=ar_r,
            device_id=(lax.div(i, 4), e, lax.rem(i, 4)), device_id_type=MESH,
        )

    def spread_one(i, carry):
        @pl.when(i != me)
        def _():
            spread(i).start()
        return carry

    lax.fori_loop(0, 16, spread_one, 0)

    b_copy.wait_recv()

    def final(c, t):
        hg_ref[0, :, c] = (t + yb[:, c].astype(F32)).astype(BF16)

    add_up(final, me, ((0, 0, width), (1, 0, width)))

    pltpu.make_async_copy(ar.at[pl.ds(0, 15)], ar.at[pl.ds(0, 15)], ar_r).wait()
    gg_ref[...] = jnp.sum(ar[...], axis=0) / gates_f

    def ring_sent(s, carry):
        for q in range(2):
            for d in range(2):
                if q == d:
                    ring_copy(d, s, q).wait_send()
                else:
                    pl.when(s < HALF)(lambda d=d, q=q: ring_copy(d, s, q).wait_send())
        y_copy(s - 1).wait_send()

        g = s - 1
        h = lax.div(g, 2)
        mine = lax.rem(g, 2) == core
        away = lax.rem(dp - lax.div(g, 4) + 4, 4)

        @pl.when(jnp.logical_not(mine))
        def _():
            core_copy(g).wait_send()

        @pl.when(mine & (away == 2))
        def _():
            x_copy(h, 0, 0, halfw).wait_send()
            x_copy(h, 1, halfw, halfw).wait_send()

        @pl.when(mine & (away == 1))
        def _():
            x_copy(h, 1, 0, width).wait_send()

        @pl.when(mine & (away == 3))
        def _():
            x_copy(h, 0, 0, width).wait_send()

        return carry

    lax.fori_loop(1, HALF + 1, ring_sent, 0)
    b_copy.wait_send()
    pltpu.make_async_copy(
        rtab.at[pl.ds(0, 2 * NZ - 1)], rtab.at[pl.ds(0, 2 * NZ - 1)], sc_s
    ).wait()
    pltpu.make_async_copy(ar.at[pl.ds(0, 15)], ar.at[pl.ds(0, 15)], ar_s).wait()


def local(dout, expert_ids, gates, down_weight, hidden_stash):
    _, width, cols = down_weight.shape
    slots = hidden_stash.shape[1]
    vmem = pl.BlockSpec(memory_space=pltpu.VMEM)
    hbm = pl.BlockSpec(memory_space=pl.ANY)
    dma = pltpu.SemaphoreType.DMA
    hg, dg, gg = pl.pallas_call(
        kernel,
        out_shape=(
            jax.ShapeDtypeStruct((1, ROWS, width), BF16),
            jax.ShapeDtypeStruct((1, width, cols), BF16),
            jax.ShapeDtypeStruct((8, TOK), F32),
        ),
        in_specs=[vmem, vmem, vmem, hbm, hbm],
        out_specs=(vmem, vmem, vmem),
        scratch_shapes=[
            pltpu.VMEM((NZ, TOK + META, cols), BF16),
            pltpu.VMEM((width, cols), BF16),
            pltpu.VMEM((slots, width), BF16),
            pltpu.VMEM((16, ROWS, cols), BF16),
            pltpu.VMEM((16, PACK, cols), BF16),
            pltpu.VMEM((16, PACK, cols), BF16),
            pltpu.VMEM((16, ROWS, cols), F32),
            pltpu.VMEM((16, ROWS, width), BF16),
            pltpu.VMEM((8, ROWS, width), BF16),
            pltpu.VMEM((8, ROWS, width), BF16),
            pltpu.VMEM((2, 8, ROWS, width), BF16),
            pltpu.VMEM((ROWS, width), BF16),
            pltpu.VMEM((16, 1, 128), F32),
            pltpu.VMEM((2 * NZ, 1, 128), F32),
            pltpu.VMEM((16, 8, TOK), F32),
            dma((2,)),
            dma((2, HALF, 2)),
            dma((2, HALF, 2)),
            dma((16,)),
            dma((16,)),
            dma((8,)),
            dma((8,)),
            dma((2, 8)),
            dma((2, 8)),
            dma(()),
            dma(()),
            dma(()),
            dma(()),
            dma(()),
            dma(()),
        ],
        compiler_params=pltpu.CompilerParams(
            collective_id=0, has_side_effects=True, vmem_limit_bytes=52 * 2**20
        ),
        cost_estimate=pl.CostEstimate(
            flops=6 * slots * width * cols, bytes_accessed=6 * 2**20, transcendentals=0
        ),
    )(dout, expert_ids.T, gates.T, down_weight[0], hidden_stash[0])
    return hg, dg, gg.T


def solution(mesh):
    in_specs = (
        P("expert", ("dp", "pipe")),
        P("expert", None),
        P("expert", None),
        P("expert", None, ("dp", "pipe")),
        P("expert", None, None),
    )
    out_specs = (
        P("expert", ("dp", "pipe"), None),
        P("expert", None, ("dp", "pipe")),
        P("expert", None),
    )
    return jax.shard_map(local, mesh=mesh, in_specs=in_specs, out_specs=out_specs, check_vma=False)
```

time: 295 us -> 128 us (0.43)
  blocking collectives: 148 us -> 0 us
  Pallas kernels: 0 us -> 121 us
  waiting for transfers between devices: 80.7 us -> 0 us
  other arithmetic: 25.4 us -> 0 us
  between operations: 14.2 us -> 0.65 us
  matrix products: 9.98 us -> 0 us
  starting transfers between devices: 7.42 us -> 0 us
  local copies, waits for them, and re-layouts: 9.03 us -> 5.5 us
    pallas_call x0 -> x1, Pallas kernels: none -> 121 us  [local(): pl.pallas_call(kernel, out_shape=(jax.ShapeDtypeStruct((1, ROWS, width),...]
    all_to_all x1 -> x0, blocking collectives: 118 us -> none  [local(): lax.all_to_all(empty.at[target].set(values).reshape(senders, local_expert...]
    all_to_all x1 -> x0, waiting for transfers between devices: 80.6 us -> none  [local(): lax.all_to_all(shaped.transpose(1, 0, 2, 3).reshape(senders, local_expert...]
    psum x1 -> x0, blocking collectives: 30.3 us -> none  [local(): gate_grad = lax.psum(partial_value, ('dp', 'pipe'))]
    another operation x3 -> x0, other arithmetic: 18.2 us -> none
    dot_general x4 -> x0, matrix products: 9.98 us -> none  [the longest x1 3.31 us: local(): jnp.einsum('erf,erd->efd', hidden_stash, routed, preferred_element_type=j...]
    all_to_all x1 -> x0, starting transfers between devices: 7.38 us -> none  [local(): lax.all_to_all(shaped.transpose(1, 0, 2, 3).reshape(senders, local_expert...]
    scatter x1 -> x0, other arithmetic: 5.59 us -> none  [local(): empty.at[target].set(values)]
  transfers between devices with their start and end apart: 2 -> 0, of which waited for: 1 -> 0; matrix products, arithmetic and copies ran while one was open for 4% -> 0% of each run, Pallas kernels for 0% -> 0%
where the time goes in v1:
time: 128 us; the launch traced here: 127 us
  Pallas kernels  121 us (95%)
  local copies, waits for them, and re-layouts  5.5 us (4%)
    pallas_call x1, Pallas kernels, local(): pl.pallas_call(kernel, out_shape=(jax.ShapeDtypeStruct((1, ROWS, width),...  121 us
    unnamed x11, local copies, waits for them, and re-layouts  5.5 us

profile of v1, /device:TPU:1, one launch (start us, length us, event | category | flops | bytes accessed | tf_op | source)
XLA Modules:
  0.0 127.3 jit_solution(1882456250337265163)
XLA Ops:
  0.6 0.0 copy-start
  0.6 1.1 copy-done
  1.8 0.0 copy-start.1
  1.8 0.8 copy-done.1
  2.6 0.0 copy-start.2
  2.6 0.7 copy-done.2
  3.3 0.0 copy-start.3
  3.3 0.7 copy-done.3
  4.0 121.1 %shard_map.76 = (bf16[1,80,1536]{2,1,0:T(8,128)(2,1)S(1)}, bf16[1,1536,256]{2,1,0:T(8,128)(2,1)S(1)}, f32[8,128]{1,0:T(8,128)S(1)}) custom-call(bf16[128,256]{1,0:T(8,128)(2,1)S(1)} %copy-done.1, s32[8,128]{1,0:T(8,128)S(1)} %bitcast.7, bf16[8,128]{1,0:T(8,128)(2,1)S(1)} %bitcast.8, bf16[1536,256]{1,0:T(8,128)(2,1)S(1)} %bitcast.6, bf16[1280,1536]{1,0:T(8,128)(2,1)} %bitcast.9), custom_call_target="tpu_custom_call" | custom-call | flops 3019898880 | bytes 6291456 | tf_op jit(solution)/shard_map/pallas_call | solution.py:431
  125.1 0.7 copy.11
  125.8 0.9 copy.12
  126.7 0.6 copy.13
Async XLA Ops:
  0.6 1.1 copy-start
  1.8 0.8 copy-start.1
  2.6 0.7 copy-start.2
  3.3 0.7 copy-start.3

commit v2 on v0

v2 whole, which is shorter than its diff:
```python
import functools

import jax
import jax.numpy as jnp
from jax import lax
from jax.experimental import pallas as pl
from jax.experimental.pallas import tpu as pltpu
from jax.sharding import PartitionSpec as P

MESH = pl.DeviceIdType.MESH
F32 = jnp.float32
BF16 = jnp.bfloat16
PAIRS = 16
NAMES = 4 * PAIRS
TOK = 128
CAP = 20
ROWS = 4 * CAP
SEG = 24
PACK = 2 * SEG
META = 16
BLOCK = 2 * TOK + META


def iota(shape, dim):
    return lax.broadcasted_iota(jnp.int32, shape, dim)


def kernel(
    dout_hbm, meta_hbm, w_hbm, st_hbm, hg_ref, dg_ref, gg_ref,
    src, w_v, st_v, sbuf, rbuf, rt, eo, pb, cr, xs, yb, xr, srow, rtab, ar,
    load_sem, ch_s, ch_r, f_s, f_r, c_s, c_r, y_s, y_r, x_s, x_r, sc_s, sc_r, ar_s, ar_r,
):
    dp, e, p = lax.axis_index("dp"), lax.axis_index("expert"), lax.axis_index("pipe")
    pair, quad = lax.div(e, 4), lax.rem(e, 4)
    yl, core = lax.div(p, 2), lax.rem(p, 2)
    me = dp * 4 + p
    width, cols = w_v.shape
    half = cols // 2

    def at_pair(d):
        return lax.rem(pair + d + PAIRS, PAIRS)

    loads = [
        pltpu.make_async_copy(dout_hbm.at[:, pl.ds(0, half)], src.at[0, pl.ds(0, TOK)], load_sem.at[0]),
        pltpu.make_async_copy(dout_hbm.at[:, pl.ds(half, half)], src.at[0, pl.ds(TOK, TOK)], load_sem.at[1]),
        pltpu.make_async_copy(meta_hbm, src.at[0, pl.ds(2 * TOK, META)], load_sem.at[2]),
        pltpu.make_async_copy(w_hbm, w_v, load_sem.at[3]),
        pltpu.make_async_copy(st_hbm, st_v, load_sem.at[4]),
    ]
    for copy in loads:
        copy.start()

    barrier = pltpu.get_barrier_semaphore()

    def greet(name):
        pl.semaphore_signal(barrier, inc=1, device_id=(dp, name, p), device_id_type=MESH)

    greet(at_pair(4) * 4 + quad)
    greet(at_pair(-4) * 4 + quad)

    def greet_near(k, carry):
        name = at_pair(lax.div(k, 4) - 2) * 4 + lax.rem(k, 4)

        @pl.when(name != e)
        def _():
            greet(name)
        return carry

    def greet_group(i, carry):
        @pl.when(i != me)
        def _():
            pl.semaphore_signal(
                barrier, inc=1, device_id=(lax.div(i, 4), e, lax.rem(i, 4)), device_id_type=MESH
            )
        return carry

    lax.fori_loop(0, 16, greet_near, 0)
    lax.fori_loop(0, 16, greet_group, 0)
    for copy in loads[:3]:
        copy.wait()
    pl.semaphore_wait(barrier, 2 + 15 + 15)

    def chain(i):
        frm, to = ((0, -4), (0, 4), (1, -4))[i - 1]
        return pltpu.make_async_remote_copy(
            src_ref=src.at[frm], dst_ref=src.at[i], send_sem=ch_s.at[i - 1], recv_sem=ch_r.at[i - 1],
            device_id=(dp, at_pair(to) * 4 + quad, p), device_id_type=MESH,
        )

    chain(1).start()
    chain(2).start()

    lower_tri = (iota((TOK, TOK), 0) < iota((TOK, TOK), 1)).astype(F32).astype(BF16)
    segment = iota((SEG, TOK), 0).astype(F32)
    row16 = iota((16, TOK), 0)
    names16 = (
        ((row16 >> 2) + (pair + PAIRS - 1)) % PAIRS * 4 + (row16 & 3)
    ).astype(F32)
    shift = (0, 4, -4, 8)

    def fill(i, k, g):
        name = at_pair(lax.div(k, 4) - 1) * 4 + lax.rem(k, 4)
        return name, pltpu.make_async_remote_copy(
            src_ref=sbuf.at[i, k], dst_ref=rbuf.at[g, quad], send_sem=f_s.at[i], recv_sem=f_r.at[g],
            device_id=(dp, name, p), device_id_type=MESH,
        )

    def select(i):
        g = at_pair(shift[i])
        x = jnp.concatenate([src[i, 0:TOK, :], src[i, TOK:2 * TOK, :]], axis=1)
        m16 = src[i, 2 * TOK:BLOCK, :].astype(F32)
        match = jnp.zeros((16, TOK), F32)
        gate = jnp.zeros((16, TOK), F32)
        for k in range(8):
            hit = m16[k:k + 1] == names16
            match = match + jnp.where(hit, 1.0, 0.0)
            gate = gate + jnp.where(hit, m16[8 + k:9 + k], 0.0)
        counts = jnp.dot(match.astype(BF16), lower_tri, preferred_element_type=F32)
        key = jnp.where(match > 0.5, counts, -1.0)
        pick = jnp.concatenate(
            [jnp.where(segment == key[k:k + 1], gate[k:k + 1], 0.0) for k in range(16)], axis=0
        ).astype(BF16)
        rows = jnp.dot(pick, x, preferred_element_type=F32)
        for k in range(16):
            r = rows[k * SEG:(k + 1) * SEG]
            sbuf[i, k] = jnp.concatenate([r[:, :half], r[:, half:]], axis=0).astype(BF16)

        def send(k, carry):
            name, copy = fill(i, k, g)

            @pl.when(name != e)
            def _():
                copy.start()
            return carry

        lax.fori_loop(0, 16, send, 0)
        pltpu.make_async_copy(sbuf.at[i, 4 + quad], rbuf.at[g, quad], f_r.at[g]).start()

    select(0)

    for copy in loads[3:]:
        copy.wait()

    def out_rows(i, carry):
        r = pl.multiple_of(i * 320, 320)
        prod = jnp.dot(st_v[pl.ds(r, 320), :], w_v[...], preferred_element_type=F32)
        eo[pl.ds(i * 4, 4)] = prod.reshape(4, ROWS, cols)
        return carry

    lax.fori_loop(0, 4, out_rows, 0)

    c_id, r_id = iota((2 * ROWS, 4 * PACK), 1), iota((2 * ROWS, 4 * PACK), 0)
    block = (
        (c_id >= PACK).astype(jnp.int32) + (c_id >= 2 * PACK).astype(jnp.int32)
        + (c_id >= 3 * PACK).astype(jnp.int32)
    )
    inside = c_id - block * PACK
    right = (inside >= SEG).astype(jnp.int32)
    slot_id = inside - right * SEG
    place = jnp.where(
        (slot_id < CAP) & (right * ROWS + block * CAP + slot_id == r_id), 1.0, 0.0
    ).astype(BF16)

    def group_of(j):
        i, r = lax.div(j, 4), lax.rem(j, 4)
        delta = jnp.where(r == 2, -1, jnp.where(r == 3, 2, r))
        off = jnp.where(i == 1, 4, jnp.where(i == 2, -4, jnp.where(i == 3, 8, 0)))
        return lax.rem(pair - delta + off + 2 * PAIRS, PAIRS)

    def core_copy(g):
        h = lax.div(g, 2)
        return pltpu.make_async_remote_copy(
            src_ref=pb.at[g], dst_ref=cr.at[h], send_sem=c_s.at[h], recv_sem=c_r.at[h],
            device_id=(dp, e, yl * 2 + (1 - core)), device_id_type=MESH,
        )

    def score_copy(g, b):
        return pltpu.make_async_remote_copy(
            src_ref=srow.at[g], dst_ref=rtab.at[e], send_sem=sc_s, recv_sem=sc_r,
            device_id=(dp, b, p), device_id_type=MESH,
        )

    diagonal = iota((ROWS, 128), 0) == iota((ROWS, 128), 1)

    def multiply(j):
        g = group_of(j)
        pltpu.make_async_copy(rbuf.at[g], rbuf.at[g], f_r.at[g]).wait()
        both = jnp.dot(place, rbuf[g].reshape(4 * PACK, half), preferred_element_type=F32)
        rr = jnp.concatenate([both[:ROWS], both[ROWS:]], axis=1).astype(BF16)
        rt[g] = rr
        for n in range(width // 256):
            part = lax.dot_general(
                rr, w_v[n * 256:(n + 1) * 256, :], (((1,), (1,)), ((), ())),
                preferred_element_type=F32,
            )
            pb[g, :, n * 256:(n + 1) * 256] = part.astype(BF16)

        @pl.when(lax.rem(g, 2) != core)
        def _():
            core_copy(g).start()

        total = jnp.sum(rr.astype(F32) * eo[g], axis=1, keepdims=True)
        srow[g] = jnp.sum(jnp.where(diagonal, total, 0.0), axis=0, keepdims=True)
        for q in range(4):
            b = 4 * g + q

            @pl.when(b != e)
            def _():
                score_copy(g, b).start()

            @pl.when(b == e)
            def _():
                rtab[e] = srow[g]

    def y_copy(h):
        return pltpu.make_async_remote_copy(
            src_ref=xs.at[h], dst_ref=yb.at[h], send_sem=y_s.at[h], recv_sem=y_r.at[h],
            device_id=(dp, e, (1 - yl) * 2 + core), device_id_type=MESH,
        )

    def x_copy(g):
        owner = lax.div(g, 4)
        place_x = jnp.maximum(lax.rem(dp - owner + 4, 4) - 1, 0)
        h = lax.div(g, 2)
        return pltpu.make_async_remote_copy(
            src_ref=xs.at[h], dst_ref=xr.at[place_x], send_sem=x_s.at[h], recv_sem=x_r.at[place_x],
            device_id=(owner, e, p), device_id_type=MESH,
        )

    def roles(g):
        mine = lax.rem(g, 2) == core
        row = lax.div(lax.rem(g, 4), 2) == yl
        return mine & jnp.logical_not(row), mine & row, mine & row & (lax.div(g, 4) != dp)

    step = width // 4

    def put_down(h, refs):
        for n in range(4):
            c = slice(n * step, (n + 1) * step)
            t = refs[0][:, c].astype(F32)
            for ref in refs[1:]:
                t = t + ref[:, c].astype(F32)
            xs[h, :, c] = t.astype(BF16)

    def along_y(j):
        g = group_of(j)
        h = lax.div(g, 2)
        gives, _, _ = roles(g)

        @pl.when(gives)
        def _():
            core_copy(g).wait_recv()
            put_down(h, (pb.at[g], cr.at[h]))
            y_copy(h).start()

    def along_x(j):
        g = group_of(j)
        h = lax.div(g, 2)
        _, keeps, passes = roles(g)

        @pl.when(keeps)
        def _():
            core_copy(g).wait_recv()
            y_copy(h).wait_recv()

        @pl.when(passes)
        def _():
            put_down(h, (pb.at[g], cr.at[h], yb.at[h]))
            x_copy(g).start()

    def body(j, carry):
        @pl.when(j == 4)
        def _():
            along_y(j - 1)
            chain(1).wait_recv()
            chain(3).start()
            select(1)
            chain(2).wait_recv()
            select(2)

        @pl.when(j == 8)
        def _():
            along_y(j - 1)
            chain(3).wait_recv()
            select(3)

        multiply(j)

        @pl.when((j != 0) & (j != 4) & (j != 8))
        def _():
            along_y(j - 1)

        @pl.when(j >= 4)
        def _():
            along_x(j - 4)

        return carry

    lax.fori_loop(0, 16, body, 0)

    def down(lo, hi):
        for n in range(lo, hi):
            part = lax.dot_general(
                st_v[:, n * 256:(n + 1) * 256], rt[...].reshape(16 * ROWS, cols),
                (((0,), (0,)), ((), ())), preferred_element_type=F32,
            )
            dg_ref[0, n * 256:(n + 1) * 256, :] = part.astype(BF16)

    along_y(15)
    down(0, 3)
    along_x(12)
    along_x(13)
    down(3, 6)
    along_x(14)
    along_x(15)

    m16 = src[0, 2 * TOK:BLOCK, :].astype(F32)
    names = iota((NAMES, TOK), 0).astype(F32)
    hits = [jnp.where(names == m16[k:k + 1, :], 1.0, 0.0) for k in range(8)]
    named = functools.reduce(lambda a, b: a + b, hits)
    counts = jnp.dot(named.astype(BF16), lower_tri, preferred_element_type=F32)
    lanes = iota((128, TOK), 0).astype(F32)
    first = (quad * CAP).astype(F32)
    pltpu.make_async_copy(
        rtab.at[pl.ds(0, NAMES - 1)], rtab.at[pl.ds(0, NAMES - 1)], sc_r
    ).wait()
    table = rtab[...].reshape(NAMES, 128)
    high = table.astype(BF16)
    low = (table - high.astype(F32)).astype(BF16)
    out = []
    for k in range(8):
        slot = jnp.sum(hits[k] * counts, axis=0, keepdims=True) + first
        one = hits[k].astype(BF16)
        values = lax.dot_general(
            high, one, (((0,), (0,)), ((), ())), preferred_element_type=F32
        ) + lax.dot_general(low, one, (((0,), (0,)), ((), ())), preferred_element_type=F32)
        out.append(jnp.sum(jnp.where(lanes == slot, values, 0.0), axis=0, keepdims=True))
    ar[me] = jnp.concatenate(out, axis=0)

    def spread_one(i, carry):
        @pl.when(i != me)
        def _():
            pltpu.make_async_remote_copy(
                src_ref=ar.at[me], dst_ref=ar.at[me], send_sem=ar_s, recv_sem=ar_r,
                device_id=(lax.div(i, 4), e, lax.rem(i, 4)), device_id_type=MESH,
            ).start()
        return carry

    lax.fori_loop(0, 16, spread_one, 0)

    for i in range(3):
        pltpu.make_async_copy(xr.at[i], xr.at[i], x_r.at[i]).wait()
    h = lax.div(me, 2)
    for n in range(4):
        c = slice(n * step, (n + 1) * step)
        t = pb[me, :, c].astype(F32)
        for ref in (cr.at[h], yb.at[h], xr.at[0], xr.at[1], xr.at[2]):
            t = t + ref[:, c].astype(F32)
        hg_ref[0, :, c] = t.astype(BF16)

    pltpu.make_async_copy(ar.at[pl.ds(0, 15)], ar.at[pl.ds(0, 15)], ar_r).wait()
    gg_ref[...] = jnp.sum(ar[...], axis=0) / m16[8:16]

    for i in range(1, 4):
        chain(i).wait_send()
    for i in range(4):
        pltpu.make_async_copy(sbuf.at[i, pl.ds(0, 15)], sbuf.at[i, pl.ds(0, 15)], f_s.at[i]).wait()

    def sent(g, carry):
        gives, _, passes = roles(g)

        @pl.when(lax.rem(g, 2) != core)
        def _():
            core_copy(g).wait_send()

        @pl.when(gives)
        def _():
            y_copy(lax.div(g, 2)).wait_send()

        @pl.when(passes)
        def _():
            x_copy(g).wait_send()

        return carry

    lax.fori_loop(0, 16, sent, 0)
    pltpu.make_async_copy(
        rtab.at[pl.ds(0, NAMES - 1)], rtab.at[pl.ds(0, NAMES - 1)], sc_s
    ).wait()
    pltpu.make_async_copy(ar.at[pl.ds(0, 15)], ar.at[pl.ds(0, 15)], ar_s).wait()


def local(dout, expert_ids, gates, down_weight, hidden_stash):
    _, width, cols = down_weight.shape
    slots = hidden_stash.shape[1]
    vmem = pl.BlockSpec(memory_space=pltpu.VMEM)
    hbm = pl.BlockSpec(memory_space=pl.ANY)
    dma = pltpu.SemaphoreType.DMA
    meta = jnp.concatenate([expert_ids.T.astype(BF16), gates.T], axis=0)
    hg, dg, gg = pl.pallas_call(
        kernel,
        out_shape=(
            jax.ShapeDtypeStruct((1, ROWS, width), BF16),
            jax.ShapeDtypeStruct((1, width, cols), BF16),
            jax.ShapeDtypeStruct((8, TOK), F32),
        ),
        in_specs=[hbm, hbm, hbm, hbm],
        out_specs=(vmem, vmem, vmem),
        scratch_shapes=[
            pltpu.VMEM((4, BLOCK, cols // 2), BF16),
            pltpu.VMEM((width, cols), BF16),
            pltpu.VMEM((slots, width), BF16),
            pltpu.VMEM((4, 16, PACK, cols // 2), BF16),
            pltpu.VMEM((PAIRS, 4, PACK, cols // 2), BF16),
            pltpu.VMEM((16, ROWS, cols), BF16),
            pltpu.VMEM((16, ROWS, cols), F32),
            pltpu.VMEM((16, ROWS, width), BF16),
            pltpu.VMEM((8, ROWS, width), BF16),
            pltpu.VMEM((8, ROWS, width), BF16),
            pltpu.VMEM((8, ROWS, width), BF16),
            pltpu.VMEM((3, ROWS, width), BF16),
            pltpu.VMEM((16, 1, 128), F32),
            pltpu.VMEM((NAMES, 1, 128), F32),
            pltpu.VMEM((16, 8, TOK), F32),
            dma((5,)),
            dma((3,)),
            dma((3,)),
            dma((4,)),
            dma((16,)),
            dma((8,)),
            dma((8,)),
            dma((8,)),
            dma((8,)),
            dma((8,)),
            dma((3,)),
            dma(()),
            dma(()),
            dma(()),
            dma(()),
        ],
        compiler_params=pltpu.CompilerParams(
            collective_id=0, has_side_effects=True, vmem_limit_bytes=60 * 2**20
        ),
        cost_estimate=pl.CostEstimate(
            flops=6 * slots * width * cols, bytes_accessed=6 * 2**20, transcendentals=0
        ),
    )(dout, meta, down_weight[0], hidden_stash[0])
    return hg, dg, gg.T


def solution(mesh):
    in_specs = (
        P("expert", ("dp", "pipe")),
        P("expert", None),
        P("expert", None),
        P("expert", None, ("dp", "pipe")),
        P("expert", None, None),
    )
    out_specs = (
        P("expert", ("dp", "pipe"), None),
        P("expert", None, ("dp", "pipe")),
        P("expert", None),
    )
    return jax.shard_map(local, mesh=mesh, in_specs=in_specs, out_specs=out_specs, check_vma=False)
```

time: 295 us -> 112 us (0.38)
  the two profiles are of different devices: /device:TPU:1 before, /device:TPU:3 now
where the time goes in v2:
time: 112 us
  Pallas kernels  105 us (94%)
  local copies, waits for them, and re-layouts  4.98 us (4%)
  other arithmetic  1.97 us (2%)
    pallas_call x1, Pallas kernels, local(): pl.pallas_call(kernel, out_shape=(jax.ShapeDtypeStruct((1, ROWS, width),...  105 us
    unnamed x3, local copies, waits for them, and re-layouts  4.98 us

profile of v2, /device:TPU:3, one launch (start us, length us, event | category | flops | bytes accessed | tf_op | source)
XLA Modules:
  0.0 112.2 jit_solution(14108400014241343048)
XLA Ops:
  0.6 0.7 convert_bitcast_fusion
  1.3 1.3 %pad_maximum_fusion.meta_hbm = bf16[16,128]{1,0:T(8,128)(2,1)} fusion(bf16[8,128]{1,0:T(8,128)(2,1)} %bitcast.7, bf16[8,128]{1,0:T(8,128)(2,1)S(1)} %convert_bitcast_fusion), kind=kLoop, calls=%fused_computation | loop fusion | flops 8192 | bytes 8192 | tf_op jit(solution)/shard_map/concatenate | solution.py:399
  2.6 104.6 %shard_map.76 = (bf16[1,80,1536]{2,1,0:T(8,128)(2,1)}, bf16[1,1536,256]{2,1,0:T(8,128)(2,1)}, f32[8,128]{1,0:T(8,128)}) custom-call(bf16[128,256]{1,0:T(8,128)(2,1)} %dout_hbm.1, bf16[16,128]{1,0:T(8,128)(2,1)} %pad_maximum_fusion.meta_hbm, bf16[1536,256]{1,0:T(8,128)(2,1)} %bitcast.9, bf16[1280,1536]{1,0:T(8,128)(2,1)} %bitcast.8), custom_call_target="tpu_custom_call" | custom-call | flops 3019898880 | bytes 6291456 | tf_op jit(solution)/shard_map/pallas_call | solution.py:400
  107.2 1.7 %copy.11 = bf16[1,80,1536]{2,1,0:T(8,128)(2,1)} copy(bf16[1,80,1536]{2,1,0:T(8,128)(2,1)} %get-tuple-element.12) | data formatting | bytes 491520
  108.9 2.1 %copy.12 = bf16[1,1536,256]{2,1,0:T(8,128)(2,1)} copy(bf16[1,1536,256]{2,1,0:T(8,128)(2,1)} %get-tuple-element.13) | data formatting | bytes 1572864
  110.9 1.3 %copy.13 = f32[128,8]{0,1:T(8,128)} copy(f32[128,8]{0,1:T(8,128)} %bitcast.6) | data formatting | bytes 8192

commit v3 on v2

--- a/solution.py
+++ b/solution.py
@@ -27,12 +27,12 @@
 
 def kernel(
     dout_hbm, meta_hbm, w_hbm, st_hbm, hg_ref, dg_ref, gg_ref,
-    src, w_v, st_v, sbuf, rbuf, rt, eo, pb, cr, xs, yb, xr, srow, rtab, ar,
+    src, w_v, st_v, sbuf, rbuf, rt, eo, pb, cr, xs, yb, xr, acc, srow, rtab, ar,
     load_sem, ch_s, ch_r, f_s, f_r, c_s, c_r, y_s, y_r, x_s, x_r, sc_s, sc_r, ar_s, ar_r,
 ):
     dp, e, p = lax.axis_index("dp"), lax.axis_index("expert"), lax.axis_index("pipe")
     pair, quad = lax.div(e, 4), lax.rem(e, 4)
-    yl, core = lax.div(p, 2), lax.rem(p, 2)
+    yh, yl, core = lax.rem(e, 2), lax.div(p, 2), lax.rem(p, 2)
     me = dp * 4 + p
     width, cols = w_v.shape
     half = cols // 2
@@ -59,7 +59,7 @@
     greet(at_pair(-4) * 4 + quad)
 
     def greet_near(k, carry):
-        name = at_pair(lax.div(k, 4) - 2) * 4 + lax.rem(k, 4)
+        name = at_pair(lax.div(k, 4) - 2 + yh) * 4 + lax.rem(k, 4)
 
         @pl.when(name != e)
         def _():
@@ -81,25 +81,27 @@
     pl.semaphore_wait(barrier, 2 + 15 + 15)
 
     def chain(i):
-        frm, to = ((0, -4), (0, 4), (1, -4))[i - 1]
+        frm, to, dst, lo, size = (
+            (0, -4, 1, 0, BLOCK), (0, 4, 2, 0, BLOCK),
+            (1, -4, 3, TOK, BLOCK - TOK), (2, 4, 3, 0, TOK),
+        )[i - 1]
         return pltpu.make_async_remote_copy(
-            src_ref=src.at[frm], dst_ref=src.at[i], send_sem=ch_s.at[i - 1], recv_sem=ch_r.at[i - 1],
+            src_ref=src.at[frm, pl.ds(lo, size)], dst_ref=src.at[dst, pl.ds(lo, size)],
+            send_sem=ch_s.at[i - 1], recv_sem=ch_r.at[i - 1],
             device_id=(dp, at_pair(to) * 4 + quad, p), device_id_type=MESH,
         )
 
-    chain(1).start()
-    chain(2).start()
 
     lower_tri = (iota((TOK, TOK), 0) < iota((TOK, TOK), 1)).astype(F32).astype(BF16)
     segment = iota((SEG, TOK), 0).astype(F32)
     row16 = iota((16, TOK), 0)
     names16 = (
-        ((row16 >> 2) + (pair + PAIRS - 1)) % PAIRS * 4 + (row16 & 3)
+        ((row16 >> 2) - (row16 & 1) + (pair + PAIRS - 1)) % PAIRS * 4 + (row16 & 3)
     ).astype(F32)
     shift = (0, 4, -4, 8)
 
     def fill(i, k, g):
-        name = at_pair(lax.div(k, 4) - 1) * 4 + lax.rem(k, 4)
+        name = at_pair(lax.div(k, 4) - 1 - lax.rem(k, 2)) * 4 + lax.rem(k, 4)
         return name, pltpu.make_async_remote_copy(
             src_ref=sbuf.at[i, k], dst_ref=rbuf.at[g, quad], send_sem=f_s.at[i], recv_sem=f_r.at[g],
             device_id=(dp, name, p), device_id_type=MESH,
@@ -134,9 +136,11 @@
             return carry
 
         lax.fori_loop(0, 16, send, 0)
-        pltpu.make_async_copy(sbuf.at[i, 4 + quad], rbuf.at[g, quad], f_r.at[g]).start()
+        pltpu.make_async_copy(sbuf.at[i, 4 * (1 + yh) + quad], rbuf.at[g, quad], f_r.at[g]).start()
 
     select(0)
+    chain(1).start()
+    chain(2).start()
 
     for copy in loads[3:]:
         copy.wait()
@@ -163,14 +167,16 @@
 
     def group_of(j):
         i, r = lax.div(j, 4), lax.rem(j, 4)
-        delta = jnp.where(r == 2, -1, jnp.where(r == 3, 2, r))
+        delta = jnp.where(r == 2, -1, jnp.where(r == 3, 2, r)) * (1 - 2 * yh)
         off = jnp.where(i == 1, 4, jnp.where(i == 2, -4, jnp.where(i == 3, 8, 0)))
         return lax.rem(pair - delta + off + 2 * PAIRS, PAIRS)
 
-    def core_copy(g):
-        h = lax.div(g, 2)
+    wide = width // 2
+
+    def core_copy(g, w):
+        h, c = lax.div(g, 2), pl.ds(w * wide, wide)
         return pltpu.make_async_remote_copy(
-            src_ref=pb.at[g], dst_ref=cr.at[h], send_sem=c_s.at[h], recv_sem=c_r.at[h],
+            src_ref=pb.at[g, :, c], dst_ref=cr.at[h, :, c], send_sem=c_s.at[h, w], recv_sem=c_r.at[h, w],
             device_id=(dp, e, yl * 2 + (1 - core)), device_id_type=MESH,
         )
 
@@ -194,10 +200,10 @@
                 preferred_element_type=F32,
             )
             pb[g, :, n * 256:(n + 1) * 256] = part.astype(BF16)
-
-        @pl.when(lax.rem(g, 2) != core)
-        def _():
-            core_copy(g).start()
+            if (n + 1) * 256 % wide == 0:
+                @pl.when(lax.rem(g, 2) != core)
+                def _():
+                    core_copy(g, n * 256 // wide).start()
 
         total = jnp.sum(rr.astype(F32) * eo[g], axis=1, keepdims=True)
         srow[g] = jnp.sum(jnp.where(diagonal, total, 0.0), axis=0, keepdims=True)
@@ -212,18 +218,21 @@
             def _():
                 rtab[e] = srow[g]
 
-    def y_copy(h):
+    def y_copy(h, w):
+        c = pl.ds(w * wide, wide)
         return pltpu.make_async_remote_copy(
-            src_ref=xs.at[h], dst_ref=yb.at[h], send_sem=y_s.at[h], recv_sem=y_r.at[h],
+            src_ref=xs.at[h, :, c], dst_ref=yb.at[h, :, c], send_sem=y_s.at[h, w], recv_sem=y_r.at[h, w],
             device_id=(dp, e, (1 - yl) * 2 + core), device_id_type=MESH,
         )
 
-    def x_copy(g):
+    def x_copy(g, w):
+        c = pl.ds(w * wide, wide)
         owner = lax.div(g, 4)
         place_x = jnp.maximum(lax.rem(dp - owner + 4, 4) - 1, 0)
         h = lax.div(g, 2)
         return pltpu.make_async_remote_copy(
-            src_ref=xs.at[h], dst_ref=xr.at[place_x], send_sem=x_s.at[h], recv_sem=x_r.at[place_x],
+            src_ref=xs.at[h, :, c], dst_ref=xr.at[place_x, :, c],
+            send_sem=x_s.at[h, w], recv_sem=x_r.at[place_x, w],
             device_id=(owner, e, p), device_id_type=MESH,
         )
 
@@ -234,8 +243,8 @@
 
     step = width // 4
 
-    def put_down(h, refs):
-        for n in range(4):
+    def put_down(h, w, refs):
+        for n in range(2 * w, 2 * w + 2):
             c = slice(n * step, (n + 1) * step)
             t = refs[0][:, c].astype(F32)
             for ref in refs[1:]:
@@ -249,44 +258,73 @@
 
         @pl.when(gives)
         def _():
-            core_copy(g).wait_recv()
-            put_down(h, (pb.at[g], cr.at[h]))
-            y_copy(h).start()
+            for w in range(2):
+                core_copy(g, w).wait_recv()
+                put_down(h, w, (pb.at[g], cr.at[h]))
+                y_copy(h, w).start()
 
     def along_x(j):
         g = group_of(j)
         h = lax.div(g, 2)
         _, keeps, passes = roles(g)
 
-        @pl.when(keeps)
-        def _():
-            core_copy(g).wait_recv()
-            y_copy(h).wait_recv()
-
-        @pl.when(passes)
-        def _():
-            put_down(h, (pb.at[g], cr.at[h], yb.at[h]))
-            x_copy(g).start()
+        for w in range(2):
+            @pl.when(keeps)
+            def _():
+                core_copy(g, w).wait_recv()
+                y_copy(h, w).wait_recv()
+
+            @pl.when(passes)
+            def _():
+                put_down(h, w, (pb.at[g], cr.at[h], yb.at[h]))
+                x_copy(g, w).start()
+
+    def down(i):
+        gs = [group_of(4 * i + r) for r in range(4)]
+        rows = jnp.concatenate([rt[g] for g in gs], axis=0)
+        for n in range(width // 256):
+            c = slice(n * 256, (n + 1) * 256)
+            stash = jnp.concatenate(
+                [st_v[pl.ds(pl.multiple_of(g * ROWS, 16), ROWS), c] for g in gs], axis=0
+            )
+            part = lax.dot_general(
+                stash, rows, (((0,), (0,)), ((), ())), preferred_element_type=F32
+            )
+            if i > 0:
+                part = part + acc[c, :]
+            if i < 3:
+                acc[c, :] = part
+            else:
+                dg_ref[0, c, :] = part.astype(BF16)
 
     def body(j, carry):
         @pl.when(j == 4)
         def _():
             along_y(j - 1)
+            down(0)
             chain(1).wait_recv()
             chain(3).start()
+            chain(2).wait_recv()
+            chain(4).start()
             select(1)
-            chain(2).wait_recv()
             select(2)
 
         @pl.when(j == 8)
         def _():
             along_y(j - 1)
+            down(1)
             chain(3).wait_recv()
+            chain(4).wait_recv()
             select(3)
 
+        @pl.when(j == 12)
+        def _():
+            along_y(j - 1)
+            down(2)
+
         multiply(j)
 
-        @pl.when((j != 0) & (j != 4) & (j != 8))
+        @pl.when((j != 0) & (j != 4) & (j != 8) & (j != 12))
         def _():
             along_y(j - 1)
 
@@ -298,21 +336,10 @@
 
     lax.fori_loop(0, 16, body, 0)
 
-    def down(lo, hi):
-        for n in range(lo, hi):
-            part = lax.dot_general(
-                st_v[:, n * 256:(n + 1) * 256], rt[...].reshape(16 * ROWS, cols),
-                (((0,), (0,)), ((), ())), preferred_element_type=F32,
-            )
-            dg_ref[0, n * 256:(n + 1) * 256, :] = part.astype(BF16)
-
     along_y(15)
-    down(0, 3)
-    along_x(12)
-    along_x(13)
-    down(3, 6)
-    along_x(14)
-    along_x(15)
+    down(3)
+    for j in range(12, 16):
+        along_x(j)
 
     m16 = src[0, 2 * TOK:BLOCK, :].astype(F32)
     names = iota((NAMES, TOK), 0).astype(F32)
@@ -348,10 +375,12 @@
 
     lax.fori_loop(0, 16, spread_one, 0)
 
-    for i in range(3):
-        pltpu.make_async_copy(xr.at[i], xr.at[i], x_r.at[i]).wait()
     h = lax.div(me, 2)
     for n in range(4):
+        if n % 2 == 0:
+            for i in range(3):
+                ref = xr.at[i, :, pl.ds(n // 2 * wide, wide)]
+                pltpu.make_async_copy(ref, ref, x_r.at[i, n // 2]).wait()
         c = slice(n * step, (n + 1) * step)
         t = pb[me, :, c].astype(F32)
         for ref in (cr.at[h], yb.at[h], xr.at[0], xr.at[1], xr.at[2]):
@@ -361,7 +390,7 @@
     pltpu.make_async_copy(ar.at[pl.ds(0, 15)], ar.at[pl.ds(0, 15)], ar_r).wait()
     gg_ref[...] = jnp.sum(ar[...], axis=0) / m16[8:16]
 
-    for i in range(1, 4):
+    for i in range(1, 5):
         chain(i).wait_send()
     for i in range(4):
         pltpu.make_async_copy(sbuf.at[i, pl.ds(0, 15)], sbuf.at[i, pl.ds(0, 15)], f_s.at[i]).wait()
@@ -369,17 +398,18 @@
     def sent(g, carry):
         gives, _, passes = roles(g)
 
-        @pl.when(lax.rem(g, 2) != core)
-        def _():
-            core_copy(g).wait_send()
-
-        @pl.when(gives)
-        def _():
-            y_copy(lax.div(g, 2)).wait_send()
-
-        @pl.when(passes)
-        def _():
-            x_copy(g).wait_send()
+        for w in range(2):
+            @pl.when(lax.rem(g, 2) != core)
+            def _():
+                core_copy(g, w).wait_send()
+
+            @pl.when(gives)
+            def _():
+                y_copy(lax.div(g, 2), w).wait_send()
+
+            @pl.when(passes)
+            def _():
+                x_copy(g, w).wait_send()
 
         return carry
 
@@ -419,20 +449,21 @@
             pltpu.VMEM((8, ROWS, width), BF16),
             pltpu.VMEM((8, ROWS, width), BF16),
             pltpu.VMEM((3, ROWS, width), BF16),
+            pltpu.VMEM((width, cols), F32),
             pltpu.VMEM((16, 1, 128), F32),
             pltpu.VMEM((NAMES, 1, 128), F32),
             pltpu.VMEM((16, 8, TOK), F32),
             dma((5,)),
-            dma((3,)),
-            dma((3,)),
+            dma((4,)),
+            dma((4,)),
             dma((4,)),
             dma((16,)),
-            dma((8,)),
-            dma((8,)),
-            dma((8,)),
-            dma((8,)),
-            dma((8,)),
-            dma((3,)),
+            dma((8, 2)),
+            dma((8, 2)),
+            dma((8, 2)),
+            dma((8, 2)),
+            dma((8, 2)),
+            dma((3, 2)),
             dma(()),
             dma(()),
             dma(()),

time: 112 us -> 104 us (0.929)
  the two profiles are of different devices: /device:TPU:3 before, /device:TPU:1 now
where the time goes in v3:
time: 104 us
  Pallas kernels  96.5 us (93%)
  local copies, waits for them, and re-layouts  4.98 us (5%)
  other arithmetic  1.97 us (2%)
    pallas_call x1, Pallas kernels, local(): pl.pallas_call(kernel, out_shape=(jax.ShapeDtypeStruct((1, ROWS, width),...  96.5 us
    unnamed x3, local copies, waits for them, and re-layouts  4.98 us

profile of v3, /device:TPU:1, one launch (start us, length us, event | category | flops | bytes accessed | tf_op | source)
XLA Modules:
  0.0 104.1 jit_solution(6177514598250145433)
XLA Ops:
  0.6 0.7 convert_bitcast_fusion
  1.3 1.3 %pad_maximum_fusion.meta_hbm = bf16[16,128]{1,0:T(8,128)(2,1)} fusion(bf16[8,128]{1,0:T(8,128)(2,1)} %bitcast.7, bf16[8,128]{1,0:T(8,128)(2,1)S(1)} %convert_bitcast_fusion), kind=kLoop, calls=%fused_computation | loop fusion | flops 8192 | bytes 8192 | tf_op jit(solution)/shard_map/concatenate | solution.py:429
  2.6 96.5 %shard_map.76 = (bf16[1,80,1536]{2,1,0:T(8,128)(2,1)}, bf16[1,1536,256]{2,1,0:T(8,128)(2,1)}, f32[8,128]{1,0:T(8,128)}) custom-call(bf16[128,256]{1,0:T(8,128)(2,1)} %dout_hbm.1, bf16[16,128]{1,0:T(8,128)(2,1)} %pad_maximum_fusion.meta_hbm, bf16[1536,256]{1,0:T(8,128)(2,1)} %bitcast.9, bf16[1280,1536]{1,0:T(8,128)(2,1)} %bitcast.8), custom_call_target="tpu_custom_call" | custom-call | flops 3019898880 | bytes 6291456 | tf_op jit(solution)/shard_map/pallas_call | solution.py:430
  99.1 1.7 %copy.11 = bf16[1,80,1536]{2,1,0:T(8,128)(2,1)} copy(bf16[1,80,1536]{2,1,0:T(8,128)(2,1)} %get-tuple-element.12) | data formatting | bytes 491520
  100.7 2.1 %copy.12 = bf16[1,1536,256]{2,1,0:T(8,128)(2,1)} copy(bf16[1,1536,256]{2,1,0:T(8,128)(2,1)} %get-tuple-element.13) | data formatting | bytes 1572864
  102.8 1.3 %copy.13 = f32[128,8]{0,1:T(8,128)} copy(f32[128,8]{0,1:T(8,128)} %bitcast.6) | data formatting | bytes 8192

commit v4 on v3

--- a/solution.py
+++ b/solution.py
@@ -26,8 +26,8 @@
 
 
 def kernel(
-    dout_hbm, meta_hbm, w_hbm, st_hbm, hg_ref, dg_ref, gg_ref,
-    src, w_v, st_v, sbuf, rbuf, rt, eo, pb, cr, xs, yb, xr, acc, srow, rtab, ar,
+    dout_hbm, ids_hbm, gates_hbm, w_hbm, st_hbm, hg_ref, dg_ref, gg_ref,
+    ids_v, gates_v, src, w_v, st_v, sbuf, rbuf, rt, eo, pb, cr, xs, yb, xr, acc, srow, rtab, ar,
     load_sem, ch_s, ch_r, f_s, f_r, c_s, c_r, y_s, y_r, x_s, x_r, sc_s, sc_r, ar_s, ar_r,
 ):
     dp, e, p = lax.axis_index("dp"), lax.axis_index("expert"), lax.axis_index("pipe")
@@ -43,7 +43,8 @@
     loads = [
         pltpu.make_async_copy(dout_hbm.at[:, pl.ds(0, half)], src.at[0, pl.ds(0, TOK)], load_sem.at[0]),
         pltpu.make_async_copy(dout_hbm.at[:, pl.ds(half, half)], src.at[0, pl.ds(TOK, TOK)], load_sem.at[1]),
-        pltpu.make_async_copy(meta_hbm, src.at[0, pl.ds(2 * TOK, META)], load_sem.at[2]),
+        pltpu.make_async_copy(ids_hbm, ids_v, load_sem.at[2]),
+        pltpu.make_async_copy(gates_hbm, gates_v, load_sem.at[5]),
         pltpu.make_async_copy(w_hbm, w_v, load_sem.at[3]),
         pltpu.make_async_copy(st_hbm, st_v, load_sem.at[4]),
     ]
@@ -76,8 +77,11 @@
 
     lax.fori_loop(0, 16, greet_near, 0)
     lax.fori_loop(0, 16, greet_group, 0)
-    for copy in loads[:3]:
+    for copy in loads[:4]:
         copy.wait()
+    src[0, 2 * TOK:BLOCK, :] = jnp.concatenate(
+        [ids_v[...].astype(F32), gates_v[...].astype(F32)], axis=0
+    ).astype(BF16)
     pl.semaphore_wait(barrier, 2 + 15 + 15)
 
     def chain(i):
@@ -142,7 +146,7 @@
     chain(1).start()
     chain(2).start()
 
-    for copy in loads[3:]:
+    for copy in loads[4:]:
         copy.wait()
 
     def out_rows(i, carry):
@@ -308,6 +312,8 @@
             chain(4).start()
             select(1)
             select(2)
+            for k in range(4):
+                along_x(k)
 
         @pl.when(j == 8)
         def _():
@@ -328,7 +334,7 @@
         def _():
             along_y(j - 1)
 
-        @pl.when(j >= 4)
+        @pl.when(j >= 8)
         def _():
             along_x(j - 4)
 
@@ -426,7 +432,6 @@
     vmem = pl.BlockSpec(memory_space=pltpu.VMEM)
     hbm = pl.BlockSpec(memory_space=pl.ANY)
     dma = pltpu.SemaphoreType.DMA
-    meta = jnp.concatenate([expert_ids.T.astype(BF16), gates.T], axis=0)
     hg, dg, gg = pl.pallas_call(
         kernel,
         out_shape=(
@@ -434,9 +439,11 @@
             jax.ShapeDtypeStruct((1, width, cols), BF16),
             jax.ShapeDtypeStruct((8, TOK), F32),
         ),
-        in_specs=[hbm, hbm, hbm, hbm],
+        in_specs=[hbm, hbm, hbm, hbm, hbm],
         out_specs=(vmem, vmem, vmem),
         scratch_shapes=[
+            pltpu.VMEM((8, TOK), jnp.int32),
+            pltpu.VMEM((8, TOK), BF16),
             pltpu.VMEM((4, BLOCK, cols // 2), BF16),
             pltpu.VMEM((width, cols), BF16),
             pltpu.VMEM((slots, width), BF16),
@@ -453,7 +460,7 @@
             pltpu.VMEM((16, 1, 128), F32),
             pltpu.VMEM((NAMES, 1, 128), F32),
             pltpu.VMEM((16, 8, TOK), F32),
-            dma((5,)),
+            dma((6,)),
             dma((4,)),
             dma((4,)),
             dma((4,)),
@@ -470,12 +477,12 @@
             dma(()),
         ],
         compiler_params=pltpu.CompilerParams(
-            collective_id=0, has_side_effects=True, vmem_limit_bytes=60 * 2**20
+            collective_id=0, has_side_effects=True, vmem_limit_bytes=50 * 2**20
         ),
         cost_estimate=pl.CostEstimate(
             flops=6 * slots * width * cols, bytes_accessed=6 * 2**20, transcendentals=0
         ),
-    )(dout, meta, down_weight[0], hidden_stash[0])
+    )(dout, expert_ids.T, gates.T, down_weight[0], hidden_stash[0])
     return hg, dg, gg.T
 
 

time: 104 us -> 102 us (0.981)
  other arithmetic: 1.97 us -> 0 us
    concatenate x1 -> x0, other arithmetic: 1.27 us -> none  [local(): meta = jnp.concatenate([expert_ids.T.astype(BF16), gates.T], axis=0)]
    unnamed x3 -> x11, local copies, waits for them, and re-layouts: 4.98 us -> 5.5 us
where the time goes in v4:
time: 102 us
  Pallas kernels  95.7 us (94%)
  local copies, waits for them, and re-layouts  5.5 us (5%)
    pallas_call x1, Pallas kernels, local(): pl.pallas_call(kernel, out_shape=(jax.ShapeDtypeStruct((1, ROWS, width),...  95.7 us
    unnamed x11, local copies, waits for them, and re-layouts  5.5 us

profile of v4, /device:TPU:1, one launch (start us, length us, event | category | flops | bytes accessed | tf_op | source)
XLA Modules:
  0.0 101.9 jit_solution(6309715160256914750)
XLA Ops:
  0.6 0.0 copy-start
  0.6 1.1 %copy-done = bf16[1,1536,256]{2,1,0:T(8,128)(2,1)S(1)} copy-done((bf16[1,1536,256]{2,1,0:T(8,128)(2,1)S(1)}, bf16[1,1536,256]{2,1,0:T(8,128)(2,1)}, u32[]{:S(2)}) %copy-start) | copy-done | bytes 786456
  1.8 0.0 copy-start.1
  1.8 0.8 copy-done.1
  2.6 0.0 copy-start.2
  2.6 0.7 copy-done.2
  3.3 0.0 copy-start.3
  3.3 0.7 copy-done.3
  4.0 95.7 %shard_map.76 = (bf16[1,80,1536]{2,1,0:T(8,128)(2,1)S(1)}, bf16[1,1536,256]{2,1,0:T(8,128)(2,1)S(1)}, f32[8,128]{1,0:T(8,128)S(1)}) custom-call(bf16[128,256]{1,0:T(8,128)(2,1)S(1)} %copy-done.1, s32[8,128]{1,0:T(8,128)S(1)} %bitcast.7, bf16[8,128]{1,0:T(8,128)(2,1)S(1)} %bitcast.8, bf16[1536,256]{1,0:T(8,128)(2,1)S(1)} %bitcast.6, bf16[1280,1536]{1,0:T(8,128)(2,1)} %bitcast.9), custom_call_target="tpu_custom_call" | custom-call | flops 3019898880 | bytes 6291456 | tf_op jit(solution)/shard_map/pallas_call | solution.py:435
  99.7 0.7 copy.11
  100.4 0.9 copy.12
  101.3 0.6 copy.13
Async XLA Ops:
  0.6 1.1 %copy-start = (bf16[1,1536,256]{2,1,0:T(8,128)(2,1)S(1)}, bf16[1,1536,256]{2,1,0:T(8,128)(2,1)}, u32[]{:S(2)}) copy-start(bf16[1,1536,256]{2,1,0:T(8,128)(2,1)} %param.8) | copy-start | bytes 2359300
  1.8 0.8 copy-start.1
  2.6 0.7 copy-start.2
  3.3 0.7 copy-start.3
